TPU v7x, 32 devices: a whole 2x2x4 slice. The times are simulated.
32 devices in a mesh: groups: 2 (over y), leaf: 8 (over z, x), sub: 2 (over core).
Axes of the slice: x: 2, y: 2, z: 4, core: 2. Of those that a mesh axis runs over, the one named last changes fastest.
Arguments:
- vectors: float32 [32, 32768], P('sub', ('groups', 'leaf')), parts along dimension 1, may hold values from -6 to 6
- points: float32 [3, 32768], P(None, ('groups', 'leaf')), parts along dimension 1, may hold values from 0 to 1
- leaf_basis: float32 [256, 64, 128], P(('groups', 'leaf')), parts along dimension 0, may hold values from -0.5 to 0.5
- local_transfer: float32 [496, 64, 64], P(('groups', 'leaf')), parts along dimension 0, may hold values from -0.5 to 0.5
- local_skeleton: float32 [480, 3, 64], P(('groups', 'leaf')), parts along dimension 0, may hold values from 0 to 1
- upper_transfer: float32 [6, 64, 64], replicated, may hold values from -0.5 to 0.5
- upper_skeleton: float32 [15, 3, 64], replicated, may hold values from 0 to 1
- near_list: int32 [2, 8192], P(None, ('groups', 'leaf')), parts along dimension 1, may hold values from 0 to 47, as said below
- far_list: int32 [2, 2048], P(None, ('groups', 'leaf')), parts along dimension 1, may hold values from 0 to 89, as said below
- upper_list: int32 [2, 256], P(None, ('groups', 'leaf')), parts along dimension 1, may hold values from 0 to 13, as said below
Outputs:
- product: float32 [32, 32768], P('sub', ('groups', 'leaf')), parts along dimension 1
There are 2 independent parts, one for each index of `groups`. A program takes and returns all parts, laid end to end along the dimension named above; an argument that names none is the same for every part. Nothing has to cross between parts.
Inputs may be any that keep to these rules, and one draw needn't show every extreme that they name: near_list[0] is a leaf of the owner, 0 to 15; near_list[1] counts leaves from the first leaf of the previous owner, 0 to 47. far_list[0] is a node of the owner below its root; far_list[1] counts nodes below the roots of owners o - 1, o, o + 1 in a row, and names a node of the same level as the row node. `upper_list`: both nodes of a pair are of the same level, never the root; an owner's pairs may name any upper nodes.
All inputs are finite; a program needn't handle non-finite values.
Results may differ from a plain program's by a relative error of at most 0.0003.
Values sent between devices are 32-bit elements; how exact they have to be, the bound alone decides.
A program may use at most 128 MiB of HBM per device.

v0:
```python
import math

import jax
import jax.numpy as jnp
from jax import lax
from jax.sharding import PartitionSpec as P

root_three = math.sqrt(3.0)
length_scale = 0.3
highest = lax.Precision.HIGHEST


def extended(cells, sides, width):
    for axis, dim in sides:
        count = lax.axis_size(axis)
        ends = count - 1
        head = lax.slice_in_dim(cells, 0, width, axis=dim)
        tail = lax.slice_in_dim(cells, cells.shape[dim] - width, cells.shape[dim], axis=dim)
        cells = jnp.concatenate(
            [
                lax.ppermute(tail, axis, [(i, (i + 1) % count) for i in range(ends)]),
                cells,
                lax.ppermute(head, axis, [((i + 1) % count, i) for i in range(ends)]),
            ],
            axis=dim,
        )
    return cells


def matern(targets, sources):
    separation = targets[..., :, :, None] - sources[..., :, None, :]
    scaled = jnp.sqrt(jnp.sum(separation * separation, axis=-3)) * (root_three / length_scale)
    return (1.0 + scaled) * jnp.exp(-scaled)


def level_table(count):
    offsets = []
    counts = []
    anchor = 0
    extent = count
    while extent >= 1:
        offsets.append(anchor)
        counts.append(extent)
        anchor += extent
        extent //= 2
    return (offsets, counts)


def pair_sum(values):
    return values.reshape((values.shape[0] // 2, 2) + values.shape[1:]).sum(axis=1)


def upsweep(leaf_coefs, transfer, offsets, counts):
    levels = [leaf_coefs]
    for height in range(len(counts) - 1):
        anchor = offsets[height]
        extent = counts[height]
        lifted = jnp.einsum(
            "nab,nvb->nva", transfer[anchor : anchor + extent], levels[-1], precision=highest
        )
        levels.append(pair_sum(lifted))
    return jnp.concatenate(levels, axis=0)


def downsweep(node_y, transfer, offsets, counts):
    for height in range(len(counts) - 2, -1, -1):
        anchor = offsets[height]
        extent = counts[height]
        above = offsets[height + 1]
        parents = jnp.repeat(node_y[above : above + counts[height + 1]], 2, axis=0)
        lowered = jnp.einsum(
            "nab,nva->nvb", transfer[anchor : anchor + extent], parents, precision=highest
        )
        node_y = node_y.at[anchor : anchor + extent].add(lowered)
    return node_y


def upper_build(root_coefs, root_lifted, upper_transfer, n_leaf):
    offsets, counts = level_table(n_leaf)
    levels = [root_coefs, pair_sum(root_lifted)]
    for height in range(1, len(counts) - 1):
        anchor = offsets[height] - n_leaf
        lifted = jnp.einsum(
            "nab,nvb->nva",
            upper_transfer[anchor : anchor + counts[height]],
            levels[-1],
            precision=highest,
        )
        levels.append(pair_sum(lifted))
    return jnp.concatenate(levels, axis=0)


def upper_down(upper_y, upper_transfer, n_leaf):
    offsets, counts = level_table(n_leaf)
    for height in range(len(counts) - 2, 0, -1):
        anchor = offsets[height]
        extent = counts[height]
        above = offsets[height + 1]
        parents = jnp.repeat(upper_y[above : above + counts[height + 1]], 2, axis=0)
        lowered = jnp.einsum(
            "nab,nva->nvb",
            upper_transfer[anchor - n_leaf : anchor - n_leaf + extent],
            parents,
            precision=highest,
        )
        upper_y = upper_y.at[anchor : anchor + extent].add(lowered)
    return upper_y


def couple(row_skeleton, col_skeleton, col_coefs, row_ids, col_ids, count):
    block_size = math.gcd(row_ids.shape[0], 256)

    def couple_add_block(running, indices):
        row_block, col_block = indices
        kernel = matern(row_skeleton[row_block], col_skeleton[col_block])
        products = jnp.einsum("gab,gvb->gva", kernel, col_coefs[col_block], precision=highest)
        return (running.at[row_block].add(products), None)

    start_value = jnp.zeros((count,) + col_coefs.shape[1:], jnp.float32)
    result, _ = lax.scan(
        couple_add_block,
        start_value,
        (row_ids.reshape(-1, block_size), col_ids.reshape(-1, block_size)),
    )
    return result


def near_field(haloed, points, row_ids, col_ids, leaf_count):
    channels = haloed.shape[0]
    leaf_size = points.shape[1] // leaf_count
    columns_all = haloed.reshape(channels, 3 * leaf_count, leaf_size)
    own_points = points.reshape(3, leaf_count, leaf_size)
    block_size = math.gcd(row_ids.shape[0], 64)

    def near_add_block(running, indices):
        row_block, col_block = indices
        sources = columns_all[:, col_block]
        kernel = matern(
            jnp.transpose(own_points[:, row_block], (1, 0, 2)),
            jnp.transpose(sources[:3], (1, 0, 2)),
        )
        products = jnp.einsum("gij,vgj->vgi", kernel, sources[3:], precision=highest)
        return (running.at[:, row_block].add(products), None)

    start_value = jnp.zeros((channels - 3, leaf_count, leaf_size), jnp.float32)
    result, _ = lax.scan(
        near_add_block,
        start_value,
        (row_ids.reshape(-1, block_size), col_ids.reshape(-1, block_size)),
    )
    return result.reshape(channels - 3, leaf_count * leaf_size)


def per_device(
    vectors,
    points,
    leaf_basis,
    local_transfer,
    local_skeleton,
    upper_transfer,
    upper_skeleton,
    near_list,
    far_list,
    upper_list,
):
    leaf_count, rank_size, leaf_size = leaf_basis.shape
    vector_count = vectors.shape[0]
    n_leaf = lax.axis_size("leaf")
    device = lax.axis_index("leaf")
    lower_count = 2 * leaf_count - 2
    offsets, counts = level_table(leaf_count)
    packed = jnp.concatenate([points, vectors], axis=0)
    haloed = extended(packed, (("leaf", 1),), vectors.shape[1])
    near_part = near_field(haloed, points, near_list[0], near_list[1], leaf_count)
    x_leaves = vectors.reshape(vector_count, leaf_count, leaf_size)
    leaf_coefs = jnp.einsum("nri,vni->nvr", leaf_basis, x_leaves, precision=highest)
    coefs = upsweep(leaf_coefs, local_transfer, offsets, counts)
    node_pack = jnp.concatenate([coefs[:lower_count], local_skeleton], axis=1)
    node_haloed = extended(node_pack, (("leaf", 0),), lower_count)
    lower_y = couple(
        local_skeleton,
        node_haloed[:, vector_count:],
        node_haloed[:, :vector_count],
        far_list[0],
        far_list[1],
        lower_count,
    )
    root_coef = coefs[lower_count]
    root_lifted = jnp.einsum("ab,vb->va", local_transfer[lower_count], root_coef, precision=highest)
    root_coefs, lifted_roots = (
        lax.all_gather(root_coef[None], "leaf", axis=0, tiled=True),
        lax.all_gather(root_lifted[None], "leaf", axis=0, tiled=True),
    )
    upper_coefs = upper_build(root_coefs, lifted_roots, upper_transfer, n_leaf)
    upper_share = couple(
        upper_skeleton, upper_skeleton, upper_coefs, upper_list[0], upper_list[1], 2 * n_leaf - 1
    )
    upper_y = lax.psum(upper_share, "leaf")
    upper_y = upper_down(upper_y, upper_transfer, n_leaf)
    own_node = lax.dynamic_index_in_dim(upper_y, device, 0, keepdims=False)
    parent_y = lax.dynamic_index_in_dim(upper_y, n_leaf + device // 2, 0, keepdims=False)
    root_y = own_node + jnp.einsum(
        "ab,va->vb", local_transfer[lower_count], parent_y, precision=highest
    )
    node_y = jnp.concatenate([lower_y, root_y[None]], axis=0)
    node_y = downsweep(node_y, local_transfer, offsets, counts)
    far_part = jnp.einsum("nri,nvr->vni", leaf_basis, node_y[:leaf_count], precision=highest)
    return near_part + far_part.reshape(vector_count, leaf_count * leaf_size)


def solution(mesh):
    return jax.shard_map(
        per_device,
        mesh=mesh,
        in_specs=(
            P("sub", ("groups", "leaf")),
            P(None, ("groups", "leaf")),
            P(("groups", "leaf"), None, None),
            P(("groups", "leaf"), None, None),
            P(("groups", "leaf"), None, None),
            P(),
            P(),
            P(None, ("groups", "leaf")),
            P(None, ("groups", "leaf")),
            P(None, ("groups", "leaf")),
        ),
        out_specs=P("sub", ("groups", "leaf")),
        check_vma=False,
    )
```

profile of v0, /device:TPU:0, one launch (start us, length us, event | category | flops | bytes accessed | tf_op | source)
XLA Modules:
  0.0 292.1 jit_solution(9327032691793521177)
XLA Ops:
  8.4 4.9 %collective-permute-start.2 = (f32[30,19,64]{2,1,0:T(8,128)S(1)}, f32[30,19,64]{2,1,0:T(8,128)S(1)}, u32[]{:S(2)}, u32[]{:S(2)}) collective-permute-start(f32[30,19,64]{2,1,0:T(8,128)S(1)} %pad_maximum_fusion.2), channel_id=1, source_target_pairs={{0,2},{2,4},{4,6},{6,8},{8,10},{10,12},{12,14},{1,3},{3,5},{5,7},{... | collective-permute-start | bytes 437768 | tf_op jit(solution)/shard_map/ppermute | solution.py:21
  15.4 5.4 %collective-permute-start = (f32[19,2048]{1,0:T(8,128)}, f32[19,2048]{1,0:T(8,128)}, u32[]{:S(2)}, u32[]{:S(2)}) collective-permute-start(f32[19,2048]{1,0:T(8,128)} %pad_maximum_fusion.3), channel_id=1, source_target_pairs={{0,2},{2,4},{4,6},{6,8},{8,10},{10,12},{12,14},{1,3},{3,5},{5,7},{... | collective-permute-start | bytes 466952 | tf_op jit(solution)/shard_map/ppermute | solution.py:21
  23.9 39.6 %all-gather = f32[128,64]{1,0:T(8,128)S(1)} all-gather(f32[16,64]{1,0:T(8,128)S(1)} %convolution_bitcast_fusion.2), channel_id=2, replica_groups=mesh['groups'=2,'leaf'=8,'sub'=2] {'leaf'}, dimensions={0}, use_global_device_ids=true | all-gather | bytes 36864 | tf_op jit(solution)/shard_map/all_gather | solution.py:191
  63.6 30.5 %all-gather.1 = f32[128,64]{1,0:T(8,128)S(1)} all-gather(f32[16,64]{1,0:T(8,128)S(1)} %fusion.46), channel_id=3, replica_groups=mesh['groups'=2,'leaf'=8,'sub'=2] {'leaf'}, dimensions={0}, use_global_device_ids=true | all-gather | bytes 36864 | tf_op jit(solution)/shard_map/all_gather | solution.py:192
  99.2 34.8 %psum.7 = f32[15,16,64]{2,1,0:T(8,128)S(1)} all-reduce(f32[15,16,64]{2,1,0:T(8,128)S(1)} %scatter_fusion.2), channel_id=1, replica_groups=mesh['groups'=2,'leaf'=8,'sub'=2] {'leaf'}, use_global_device_ids=true, to_apply=%region_13.14 | all-reduce | flops 15360 | bytes 122880 | tf_op jit(solution)/shard_map/psum | solution.py:198
  139.4 4.5 %copy.35 = f32[128,64,64]{2,1,0:T(8,128)} copy(f32[128,64,64]{0,2,1:T(8,128)S(1)} %exponential_multiply_fusion) | data formatting | bytes 4194304 | tf_op jit(solution)/shard_map/while/body/eval_jaxpr/mul | solution.py:33
  145.8 8.3 %fusion.61 = f32[128,16,64]{2,1,0:T(8,128)S(1)} fusion(f32[128,16,64]{2,1,0:T(8,128)S(1)} %gather_fusion.2, f32[128,64,64]{2,1,0:T(8,128)} %copy.35), kind=kOutput, calls=%fused_computation.114 | convolution fusion | flops 100663296 | bytes 3145728 | tf_op jit(solution)/shard_map/while/body/eval_jaxpr/gab,gvb->gva/dot_general | solution.py:116
  154.2 5.2 %scatter_fusion.1 = f32[30,16,64]{2,1,0:T(8,128)S(1)} fusion(f32[30,16,64]{2,1,0:T(8,128)S(1)} %broadcast_in_dim.42, s32[128]{0:T(128)S(1)} %get-tuple-element.180, f32[128,16,64]{2,1,0:T(8,128)S(1)} %fusion.61), kind=kCustom, calls=%fused_computation.9 | custom fusion | flops 131072 | bytes 1573376 | tf_op jit(solution)/shard_map/while/body/eval_jaxpr/scatter-add | solution.py:117
  162.2 128.7 %while.24 = (s32[]{:T(128)}, f32[16,16,128]{2,0,1:T(8,128)S(1)}, s32[8,64]{1,0:T(8,128)S(1)}, s32[8,64]{1,0:T(8,128)S(1)}, f32[19,48,128]{2,0,1:T(8,128)S(1)}, /*index=5*/f32[3,16,128]{2,0,1:T(4,128)S(1)}, s32[]{:T(128)}) while((s32[]{:T(128)}, f32[16,16,128]{2,0,1:T(8,128)S(1)}, s32[8,64]{1,0:T(8,128)S(1)}, s32[8,64]{1,0:T(8,128)S(1)}, ...), condition=%wide.region_3.4_spmd, body=%wide.region_0.3_spmd.sunk | while | flops 214043008 | bytes 12855633 | solution.py:146
  163.8 4.1 %multiply_reduce_fusion.4 = f32[64,128,128]{2,1,0:T(8,128)S(1)} fusion(f32[64,3,128]{2,1,0:T(4,128)S(1)} %slice_bitcast_fusion.3, f32[64,3,128]{2,1,0:T(4,128)S(1)} %gather_fusion.1), kind=kLoop, calls=%fused_computation.11.clone.1 | loop fusion | flops 8388608 | bytes 4390912 | tf_op jit(solution)/shard_map/while/body/eval_jaxpr/reduce_sum | solution.py:32
  167.9 7.6 %fusion.87 = f32[64,16,128]{2,1,0:T(8,128)S(1)} fusion(f32[64,128,128]{2,1,0:T(8,128)S(1)} %multiply_reduce_fusion.4, f32[19,64,128]{2,0,1:T(8,128)S(1)} %bitcast.106), kind=kOutput, calls=%fused_computation.12.clone.1 | convolution fusion | flops 205520896 | bytes 5242880 | tf_op jit(solution)/shard_map/while/body/eval_jaxpr/gij,vgj->vgi/dot_general | solution.py:142
  175.5 2.9 %scatter_fusion = f32[16,16,128]{2,0,1:T(8,128)S(1)} fusion(f32[16,16,128]{2,0,1:T(8,128)S(1)} %get-tuple-element.230, s32[64]{0:T(128)S(1)} %get-tuple-element.220, f32[64,16,128]{2,1,0:T(8,128)S(1)} %fusion.87), kind=kCustom, calls=%fused_computation.8.clone.1 | custom fusion | flops 131072 | bytes 1573120 | tf_op jit(solution)/shard_map/while/body/eval_jaxpr/scatter-add | solution.py:143
  179.9 4.1 %multiply_reduce_fusion.4 = f32[64,128,128]{2,1,0:T(8,128)S(1)} fusion(f32[64,3,128]{2,1,0:T(4,128)S(1)} %slice_bitcast_fusion.3, f32[64,3,128]{2,1,0:T(4,128)S(1)} %gather_fusion.1), kind=kLoop, calls=%fused_computation.11.clone.1 | loop fusion | flops 8388608 | bytes 4390912 | tf_op jit(solution)/shard_map/while/body/eval_jaxpr/reduce_sum | solution.py:32
  184.0 7.6 %fusion.87 = f32[64,16,128]{2,1,0:T(8,128)S(1)} fusion(f32[64,128,128]{2,1,0:T(8,128)S(1)} %multiply_reduce_fusion.4, f32[19,64,128]{2,0,1:T(8,128)S(1)} %bitcast.106), kind=kOutput, calls=%fused_computation.12.clone.1 | convolution fusion | flops 205520896 | bytes 5242880 | tf_op jit(solution)/shard_map/while/body/eval_jaxpr/gij,vgj->vgi/dot_general | solution.py:142
  191.6 2.9 %scatter_fusion = f32[16,16,128]{2,0,1:T(8,128)S(1)} fusion(f32[16,16,128]{2,0,1:T(8,128)S(1)} %get-tuple-element.230, s32[64]{0:T(128)S(1)} %get-tuple-element.220, f32[64,16,128]{2,1,0:T(8,128)S(1)} %fusion.87), kind=kCustom, calls=%fused_computation.8.clone.1 | custom fusion | flops 131072 | bytes 1573120 | tf_op jit(solution)/shard_map/while/body/eval_jaxpr/scatter-add | solution.py:143
  195.9 4.1 %multiply_reduce_fusion.4 = f32[64,128,128]{2,1,0:T(8,128)S(1)} fusion(f32[64,3,128]{2,1,0:T(4,128)S(1)} %slice_bitcast_fusion.3, f32[64,3,128]{2,1,0:T(4,128)S(1)} %gather_fusion.1), kind=kLoop, calls=%fused_computation.11.clone.1 | loop fusion | flops 8388608 | bytes 4390912 | tf_op jit(solution)/shard_map/while/body/eval_jaxpr/reduce_sum | solution.py:32
  200.1 7.6 %fusion.87 = f32[64,16,128]{2,1,0:T(8,128)S(1)} fusion(f32[64,128,128]{2,1,0:T(8,128)S(1)} %multiply_reduce_fusion.4, f32[19,64,128]{2,0,1:T(8,128)S(1)} %bitcast.106), kind=kOutput, calls=%fused_computation.12.clone.1 | convolution fusion | flops 205520896 | bytes 5242880 | tf_op jit(solution)/shard_map/while/body/eval_jaxpr/gij,vgj->vgi/dot_general | solution.py:142
  207.7 2.9 %scatter_fusion = f32[16,16,128]{2,0,1:T(8,128)S(1)} fusion(f32[16,16,128]{2,0,1:T(8,128)S(1)} %get-tuple-element.230, s32[64]{0:T(128)S(1)} %get-tuple-element.220, f32[64,16,128]{2,1,0:T(8,128)S(1)} %fusion.87), kind=kCustom, calls=%fused_computation.8.clone.1 | custom fusion | flops 131072 | bytes 1573120 | tf_op jit(solution)/shard_map/while/body/eval_jaxpr/scatter-add | solution.py:143
  212.0 4.1 %multiply_reduce_fusion.4 = f32[64,128,128]{2,1,0:T(8,128)S(1)} fusion(f32[64,3,128]{2,1,0:T(4,128)S(1)} %slice_bitcast_fusion.3, f32[64,3,128]{2,1,0:T(4,128)S(1)} %gather_fusion.1), kind=kLoop, calls=%fused_computation.11.clone.1 | loop fusion | flops 8388608 | bytes 4390912 | tf_op jit(solution)/shard_map/while/body/eval_jaxpr/reduce_sum | solution.py:32
  216.1 7.6 %fusion.87 = f32[64,16,128]{2,1,0:T(8,128)S(1)} fusion(f32[64,128,128]{2,1,0:T(8,128)S(1)} %multiply_reduce_fusion.4, f32[19,64,128]{2,0,1:T(8,128)S(1)} %bitcast.106), kind=kOutput, calls=%fused_computation.12.clone.1 | convolution fusion | flops 205520896 | bytes 5242880 | tf_op jit(solution)/shard_map/while/body/eval_jaxpr/gij,vgj->vgi/dot_general | solution.py:142
  223.7 2.9 %scatter_fusion = f32[16,16,128]{2,0,1:T(8,128)S(1)} fusion(f32[16,16,128]{2,0,1:T(8,128)S(1)} %get-tuple-element.230, s32[64]{0:T(128)S(1)} %get-tuple-element.220, f32[64,16,128]{2,1,0:T(8,128)S(1)} %fusion.87), kind=kCustom, calls=%fused_computation.8.clone.1 | custom fusion | flops 131072 | bytes 1573120 | tf_op jit(solution)/shard_map/while/body/eval_jaxpr/scatter-add | solution.py:143
  228.0 4.1 %multiply_reduce_fusion.4 = f32[64,128,128]{2,1,0:T(8,128)S(1)} fusion(f32[64,3,128]{2,1,0:T(4,128)S(1)} %slice_bitcast_fusion.3, f32[64,3,128]{2,1,0:T(4,128)S(1)} %gather_fusion.1), kind=kLoop, calls=%fused_computation.11.clone.1 | loop fusion | flops 8388608 | bytes 4390912 | tf_op jit(solution)/shard_map/while/body/eval_jaxpr/reduce_sum | solution.py:32
  232.2 7.6 %fusion.87 = f32[64,16,128]{2,1,0:T(8,128)S(1)} fusion(f32[64,128,128]{2,1,0:T(8,128)S(1)} %multiply_reduce_fusion.4, f32[19,64,128]{2,0,1:T(8,128)S(1)} %bitcast.106), kind=kOutput, calls=%fused_computation.12.clone.1 | convolution fusion | flops 205520896 | bytes 5242880 | tf_op jit(solution)/shard_map/while/body/eval_jaxpr/gij,vgj->vgi/dot_general | solution.py:142
  239.8 2.9 %scatter_fusion = f32[16,16,128]{2,0,1:T(8,128)S(1)} fusion(f32[16,16,128]{2,0,1:T(8,128)S(1)} %get-tuple-element.230, s32[64]{0:T(128)S(1)} %get-tuple-element.220, f32[64,16,128]{2,1,0:T(8,128)S(1)} %fusion.87), kind=kCustom, calls=%fused_computation.8.clone.1 | custom fusion | flops 131072 | bytes 1573120 | tf_op jit(solution)/shard_map/while/body/eval_jaxpr/scatter-add | solution.py:143
  244.1 4.1 %multiply_reduce_fusion.4 = f32[64,128,128]{2,1,0:T(8,128)S(1)} fusion(f32[64,3,128]{2,1,0:T(4,128)S(1)} %slice_bitcast_fusion.3, f32[64,3,128]{2,1,0:T(4,128)S(1)} %gather_fusion.1), kind=kLoop, calls=%fused_computation.11.clone.1 | loop fusion | flops 8388608 | bytes 4390912 | tf_op jit(solution)/shard_map/while/body/eval_jaxpr/reduce_sum | solution.py:32
  248.2 7.6 %fusion.87 = f32[64,16,128]{2,1,0:T(8,128)S(1)} fusion(f32[64,128,128]{2,1,0:T(8,128)S(1)} %multiply_reduce_fusion.4, f32[19,64,128]{2,0,1:T(8,128)S(1)} %bitcast.106), kind=kOutput, calls=%fused_computation.12.clone.1 | convolution fusion | flops 205520896 | bytes 5242880 | tf_op jit(solution)/shard_map/while/body/eval_jaxpr/gij,vgj->vgi/dot_general | solution.py:142
  255.8 2.9 %scatter_fusion = f32[16,16,128]{2,0,1:T(8,128)S(1)} fusion(f32[16,16,128]{2,0,1:T(8,128)S(1)} %get-tuple-element.230, s32[64]{0:T(128)S(1)} %get-tuple-element.220, f32[64,16,128]{2,1,0:T(8,128)S(1)} %fusion.87), kind=kCustom, calls=%fused_computation.8.clone.1 | custom fusion | flops 131072 | bytes 1573120 | tf_op jit(solution)/shard_map/while/body/eval_jaxpr/scatter-add | solution.py:143
  260.1 4.1 %multiply_reduce_fusion.4 = f32[64,128,128]{2,1,0:T(8,128)S(1)} fusion(f32[64,3,128]{2,1,0:T(4,128)S(1)} %slice_bitcast_fusion.3, f32[64,3,128]{2,1,0:T(4,128)S(1)} %gather_fusion.1), kind=kLoop, calls=%fused_computation.11.clone.1 | loop fusion | flops 8388608 | bytes 4390912 | tf_op jit(solution)/shard_map/while/body/eval_jaxpr/reduce_sum | solution.py:32
  264.3 7.6 %fusion.87 = f32[64,16,128]{2,1,0:T(8,128)S(1)} fusion(f32[64,128,128]{2,1,0:T(8,128)S(1)} %multiply_reduce_fusion.4, f32[19,64,128]{2,0,1:T(8,128)S(1)} %bitcast.106), kind=kOutput, calls=%fused_computation.12.clone.1 | convolution fusion | flops 205520896 | bytes 5242880 | tf_op jit(solution)/shard_map/while/body/eval_jaxpr/gij,vgj->vgi/dot_general | solution.py:142
  271.9 2.9 %scatter_fusion = f32[16,16,128]{2,0,1:T(8,128)S(1)} fusion(f32[16,16,128]{2,0,1:T(8,128)S(1)} %get-tuple-element.230, s32[64]{0:T(128)S(1)} %get-tuple-element.220, f32[64,16,128]{2,1,0:T(8,128)S(1)} %fusion.87), kind=kCustom, calls=%fused_computation.8.clone.1 | custom fusion | flops 131072 | bytes 1573120 | tf_op jit(solution)/shard_map/while/body/eval_jaxpr/scatter-add | solution.py:143
  276.2 4.1 %multiply_reduce_fusion.4 = f32[64,128,128]{2,1,0:T(8,128)S(1)} fusion(f32[64,3,128]{2,1,0:T(4,128)S(1)} %slice_bitcast_fusion.3, f32[64,3,128]{2,1,0:T(4,128)S(1)} %gather_fusion.1), kind=kLoop, calls=%fused_computation.11.clone.1 | loop fusion | flops 8388608 | bytes 4390912 | tf_op jit(solution)/shard_map/while/body/eval_jaxpr/reduce_sum | solution.py:32
  280.3 7.6 %fusion.87 = f32[64,16,128]{2,1,0:T(8,128)S(1)} fusion(f32[64,128,128]{2,1,0:T(8,128)S(1)} %multiply_reduce_fusion.4, f32[19,64,128]{2,0,1:T(8,128)S(1)} %bitcast.106), kind=kOutput, calls=%fused_computation.12.clone.1 | convolution fusion | flops 205520896 | bytes 5242880 | tf_op jit(solution)/shard_map/while/body/eval_jaxpr/gij,vgj->vgi/dot_general | solution.py:142
  (143 shorter events, 43.2 us)
Async XLA Ops:
  0.0 1.0 copy-start
  0.0 14.6 %copy-start.6 = (f32[16,2048]{1,0:T(8,128)S(1)}, f32[16,2048]{1,0:T(8,128)}, u32[]{:S(2)}) copy-start(f32[16,2048]{1,0:T(8,128)} %param.24) | copy-start | bytes 393220
  0.0 14.6 %copy-start.3 = (f32[3,2048]{1,0:T(4,128)S(1)}, f32[3,2048]{1,0:T(4,128)}, u32[]{:S(2)}) copy-start(f32[3,2048]{1,0:T(4,128)} %param.25) | copy-start | bytes 73732
  0.0 63.6 %copy-start.11 = (s32[2,128]{1,0:T(2,128)S(1)}, s32[2,128]{1,0:T(2,128)}, u32[]{:S(2)}) copy-start(s32[2,128]{1,0:T(2,128)} %param.32) | copy-start | bytes 3076
  0.0 94.1 %copy-start.9 = (f32[6,64,64]{2,1,0:T(8,128)S(1)}, f32[6,64,64]{2,1,0:T(8,128)}, u32[]{:S(2)}) copy-start(f32[6,64,64]{2,1,0:T(8,128)} %param.29) | copy-start | bytes 294916
  0.0 94.6 %copy-start.12 = (s32[2,16]{1,0:T(2,128)S(1)}, s32[2,16]{1,0:T(2,128)}, u32[]{:S(2)}) copy-start(s32[2,16]{1,0:T(2,128)} %param.33) | copy-start | bytes 388
  0.0 95.2 %copy-start.2 = (f32[15,3,64]{2,0,1:T(8,128)S(1)}, f32[15,3,64]{2,0,1:T(8,128)}, u32[]{:S(2)}) copy-start(f32[15,3,64]{2,0,1:T(8,128)} %param.30) | copy-start | bytes 34564
  8.4 128.2 %copy-start.7 = (f32[30,3,64]{2,1,0:T(4,128)}, f32[30,3,64]{2,1,0:T(4,128)S(1)}, u32[]{:S(2)}) copy-start(f32[30,3,64]{2,1,0:T(4,128)S(1)} %copy.32) | copy-start | bytes 69124
  8.4 128.2 %collective-permute-start.2 = (f32[30,19,64]{2,1,0:T(8,128)S(1)}, f32[30,19,64]{2,1,0:T(8,128)S(1)}, u32[]{:S(2)}, u32[]{:S(2)}) collective-permute-start(f32[30,19,64]{2,1,0:T(8,128)S(1)} %pad_maximum_fusion.2), channel_id=1, source_target_pairs={{0,2},{2,4},{4,6},{6,8},{8,10},{10,12},{12,14},{1,3},{3,5},{5,7},{... | collective-permute-start | bytes 437768 | tf_op jit(solution)/shard_map/ppermute | solution.py:21
  13.3 123.3 %collective-permute-start.3 = (f32[30,19,64]{2,1,0:T(8,128)S(1)}, f32[30,19,64]{2,1,0:T(8,128)S(1)}, u32[]{:S(2)}, u32[]{:S(2)}) collective-permute-start(f32[30,19,64]{2,1,0:T(8,128)S(1)} %pad_maximum_fusion.2), channel_id=1, source_target_pairs={{2,0},{4,2},{6,4},{8,6},{10,8},{12,10},{14,12},{3,1},{5,3},{7,5},{... | collective-permute-start | bytes 437768 | tf_op jit(solution)/shard_map/ppermute | solution.py:23
  15.3 118.9 %copy-start.10 = (s32[2,512]{1,0:T(2,128)S(1)}, s32[2,512]{1,0:T(2,128)}, u32[]{:S(2)}) copy-start(s32[2,512]{1,0:T(2,128)} %param.31) | copy-start | bytes 12292
  15.4 145.4 %collective-permute-start = (f32[19,2048]{1,0:T(8,128)}, f32[19,2048]{1,0:T(8,128)}, u32[]{:S(2)}, u32[]{:S(2)}) collective-permute-start(f32[19,2048]{1,0:T(8,128)} %pad_maximum_fusion.3), channel_id=1, source_target_pairs={{0,2},{2,4},{4,6},{6,8},{8,10},{10,12},{12,14},{1,3},{3,5},{5,7},{... | collective-permute-start | bytes 466952 | tf_op jit(solution)/shard_map/ppermute | solution.py:21
  20.7 140.1 %collective-permute-start.1 = (f32[19,2048]{1,0:T(8,128)}, f32[19,2048]{1,0:T(8,128)}, u32[]{:S(2)}, u32[]{:S(2)}) collective-permute-start(f32[19,2048]{1,0:T(8,128)} %pad_maximum_fusion.3), channel_id=1, source_target_pairs={{2,0},{4,2},{6,4},{8,6},{10,8},{12,10},{14,12},{3,1},{5,3},{7,5},{... | collective-permute-start | bytes 466952 | tf_op jit(solution)/shard_map/ppermute | solution.py:23
  94.1 41.3 %copy-start.1 = (f32[30,3,64]{2,0,1:T(8,128)S(1)}, f32[30,3,64]{2,0,1:T(8,128)}, u32[]{:S(2)}) copy-start(f32[30,3,64]{2,0,1:T(8,128)} %param.28) | copy-start | bytes 69124
  136.6 0.9 copy-start.5
  139.4 4.5 %copy-start.8 = (f32[30,3,64]{2,1,0:T(4,128)S(1)}, f32[30,3,64]{2,1,0:T(4,128)}, u32[]{:S(2)}) copy-start(f32[30,3,64]{2,1,0:T(4,128)} %copy-done.7) | copy-start | bytes 69124
  154.1 5.3 %copy-start.4 = (f32[31,64,64]{2,1,0:T(8,128)S(1)}, f32[31,64,64]{2,1,0:T(8,128)}, u32[]{:S(2)}) copy-start(f32[31,64,64]{2,1,0:T(8,128)} %param.27) | copy-start | bytes 1523716
where the time goes:
time: 293 us; the launch traced here: 292 us
  blocking collectives  105 us (36%)
  matrix products  82.1 us (28%)
  other arithmetic  68.3 us (23%)
  local copies, waits for them, and re-layouts  22.5 us (8%)
  starting transfers between devices  12.8 us (4%)
    dot_general x8, matrix products, near_add_block(): jnp.einsum('gij,vgj->vgi', kernel, sources[3:], precision=highest)  60.8 us
    all_gather x1, blocking collectives, per_device(): lax.all_gather(root_coef[None], 'leaf', axis=0, tiled=True)  39.6 us
    psum x1, blocking collectives, per_device(): upper_y = lax.psum(upper_share, 'leaf')  34.8 us
    reduce_sum x10, other arithmetic, matern(): jnp.sum(separation * separation, axis=-3)  34.4 us
    all_gather x1, blocking collectives, per_device(): lax.all_gather(root_lifted[None], 'leaf', axis=0, tiled=True)  30.5 us
    scatter-add x8, other arithmetic, near_add_block(): return (running.at[:, row_block].add(products), None)  23.4 us
    ppermute x2, starting transfers between devices, extended(): lax.ppermute(tail, axis, [(i, (i + 1) % count) for i in range(ends)])  10.2 us
    dot_general x2, matrix products, couple_add_block(): jnp.einsum('gab,gvb->gva', kernel, col_coefs[col_block], precision=highest)  9.39 us
  transfers between devices with their start and end apart: 4, of which 0 were waited for; matrix products, arithmetic and copies ran while one was open for 12% of the time, Pallas kernels for 0%

commit v1 on v0

v1 whole, which is shorter than its diff:
```python
import functools
import math

import jax
import jax.numpy as jnp
from jax import lax
from jax.experimental import pallas as pl
from jax.experimental.pallas import tpu as pltpu
from jax.sharding import PartitionSpec as P

root_three = math.sqrt(3.0)
length_scale = 0.3
log2e = math.log2(math.e)
ln2 = math.log(2.0)
point_scale = root_three / length_scale * log2e
highest = lax.Precision.HIGHEST
MESH = pl.DeviceIdType.MESH
FEATURES = 32
GROUP = 4
f32 = jnp.float32
bf16 = jnp.bfloat16


def level_table(count):
    offsets = []
    counts = []
    anchor = 0
    extent = count
    while extent >= 1:
        offsets.append(anchor)
        counts.append(extent)
        anchor += extent
        extent //= 2
    return (offsets, counts)


def dot_nt(a, b):
    return lax.dot_general(
        a, b, (((1,), (1,)), ((), ())), precision=highest, preferred_element_type=f32
    )


def dot_nn(a, b):
    return lax.dot_general(
        a, b, (((1,), (0,)), ((), ())), precision=highest, preferred_element_type=f32
    )


def dot_fast(a, b):
    return lax.dot_general(a, b, (((1,), (0,)), ((), ())), preferred_element_type=f32)


def each(start, stop, body):
    if stop - start <= 16:
        for i in range(start, stop):
            body(i)
    else:

        @pl.loop(start, stop)
        def _(i):
            body(i)


def exchange_kernel(
    n,
    halo_width,
    x_ref,
    pts_ref,
    basis_ref,
    tr_ref,
    ulist_ref,
    nlist_ref,
    xall,
    ptsall,
    call,
    roots,
    cols_out,
    wts_out,
    halo_send,
    halo_recv,
    root_send,
    root_recv,
):
    me = lax.axis_index("leaf")
    leaf_count, rank, leaf = basis_ref.shape
    vecs = x_ref.shape[0]
    lower = 2 * leaf_count - 2
    offsets, counts = level_table(leaf_count)
    entries = ulist_ref.shape[1]

    barrier = pltpu.get_barrier_semaphore()

    def greet(d):
        pl.semaphore_signal(
            barrier, inc=1, device_id={"leaf": lax.rem(me + d, n)}, device_id_type=MESH
        )

    each(1, n, greet)
    pl.semaphore_wait(barrier, n - 1)

    own_pts = pts_ref.at[:, pl.ds(0, halo_width)]
    own_coefs = call.at[pl.ds(lower, lower)]
    sources = (x_ref, own_pts, own_coefs)

    def halo(kind, side):
        slot = 2 * side
        target = (xall.at[slot], ptsall.at[slot], call.at[pl.ds(slot * lower, lower)])[kind]
        other = jnp.minimum(me + 1, n - 1) if side == 0 else jnp.maximum(me - 1, 0)
        return pltpu.make_async_remote_copy(
            src_ref=sources[kind],
            dst_ref=target,
            send_sem=halo_send.at[kind, side],
            recv_sem=halo_recv.at[kind, side],
            device_id={"leaf": other},
            device_id_type=MESH,
        )

    def sends(side):
        return me < n - 1 if side == 0 else me > 0

    def receives(side):
        return me > 0 if side == 0 else me < n - 1

    for side in range(2):

        @pl.when(sends(side))
        def _():
            halo(0, side).start()
            halo(1, side).start()

    def up(node):
        return dot_nt(call[lower + node], tr_ref[node])

    for i in range(leaf_count):
        call[lower + i] = dot_nt(x_ref[:, i * leaf : (i + 1) * leaf], basis_ref[i])
    for height in range(1, len(counts) - 1):
        below = offsets[height - 1]
        for j in range(counts[height]):
            call[lower + offsets[height] + j] = up(below + 2 * j) + up(below + 2 * j + 1)
    for side in range(2):

        @pl.when(sends(side))
        def _():
            halo(2, side).start()

    root = up(lower - 2) + up(lower - 1)
    roots[me] = jnp.zeros(roots.shape[1:], f32)
    roots[me, 0:vecs, 0:rank] = root
    roots[me, 0:vecs, rank : 2 * rank] = dot_nt(root, tr_ref[lower])
    roots[me, vecs : vecs + 2, 0:entries] = ulist_ref[...].astype(f32)

    def root_copy(d):
        return pltpu.make_async_remote_copy(
            src_ref=roots.at[me],
            dst_ref=roots.at[me],
            send_sem=root_send.at[d],
            recv_sem=root_recv.at[d],
            device_id={"leaf": lax.rem(me + d, n)},
            device_id_type=MESH,
        )

    def root_arrival(d):
        sender = lax.rem(me + n - d, n)
        return pltpu.make_async_remote_copy(
            src_ref=roots.at[me],
            dst_ref=roots.at[sender],
            send_sem=root_send.at[d],
            recv_sem=root_recv.at[d],
            device_id={"leaf": lax.rem(me + d, n)},
            device_id_type=MESH,
        )

    each(1, n, lambda d: root_copy(d).start())

    xall[1] = x_ref[...]
    ptsall[1] = pts_ref[:, 0:halo_width]
    for side in range(2):
        slot = 2 * side

        @pl.when(jnp.logical_not(receives(side)))
        def _():
            xall[slot] = jnp.zeros(xall.shape[1:], f32)
            ptsall[slot] = jnp.zeros(ptsall.shape[1:], f32)
            call[slot * lower : (slot + 1) * lower] = jnp.zeros((lower,) + call.shape[1:], f32)

    total = nlist_ref.shape[1]
    row_hot = (
        lax.broadcasted_iota(jnp.int32, (leaf_count, total), 0) == nlist_ref[0:1, :]
    ).astype(f32).astype(bf16)
    col_hot = (
        lax.broadcasted_iota(jnp.int32, (128, total), 0) == nlist_ref[1:2, :]
    ).astype(f32).astype(bf16)
    count = lax.dot_general(
        row_hot, col_hot, (((1,), (1,)), ((), ())), preferred_element_type=f32
    )
    has = (count > 0.5).astype(f32)
    before = (
        lax.broadcasted_iota(jnp.int32, (128, 128), 0)
        < lax.broadcasted_iota(jnp.int32, (128, 128), 1)
    ).astype(f32).astype(bf16)
    place = dot_fast(has.astype(bf16), before)
    place = jnp.where(has > 0.5, place, -1.0)
    lane = lax.broadcasted_iota(jnp.int32, (leaf_count, 128), 1)
    lane_f = lane.astype(f32)
    cols = jnp.zeros((leaf_count, 128), f32)
    wts = jnp.zeros((leaf_count, 128), f32)
    for c in range(3 * leaf_count):
        hit = place[:, c : c + 1] == lane_f
        cols = cols + jnp.where(hit, float(c), 0.0)
        wts = wts + jnp.where(hit, count[:, c : c + 1], 0.0)
    filled = jnp.sum(has, axis=1, keepdims=True)
    cols_out[...] = jnp.where(lane == 127, filled, cols).astype(jnp.int32)
    wts_out[...] = wts * ln2

    for side in range(2):

        @pl.when(sends(side))
        def _():
            for kind in range(3):
                halo(kind, side).wait_send()

        @pl.when(receives(side))
        def _():
            for kind in range(3):
                halo(kind, side).wait_recv()

    def finish(d):
        root_copy(d).wait_send()
        root_arrival(d).wait_recv()

    each(1, n, finish)


def split(values):
    high = values.astype(bf16)
    return high, (values - high.astype(f32)).astype(bf16)


def kernel_values(squared):
    squared = jnp.maximum(squared, 1e-20)
    t = squared * lax.rsqrt(squared)
    return (t + log2e) * jnp.exp2(-t)


def product(values, kernel):
    kernel_high, kernel_low = split(kernel)
    high, low = split(values)
    rows = values.shape[0]
    both = dot_fast(jnp.concatenate([high, low], axis=0), kernel_high)
    return both[:rows] + both[rows:] + dot_fast(high, kernel_low)


def couple_kernel(
    n,
    entries,
    cols_ref,
    wts_ref,
    far_ref,
    xall,
    ptsall,
    uppts_ref,
    call,
    roots,
    basis_ref,
    tr_ref,
    uptr_ref,
    out_ref,
    feat,
    near_t,
    near_row,
    skel_t,
    skel_row,
    up_t,
    up_row,
    y_ref,
    upc,
):
    me = lax.axis_index("leaf")
    leaf_count, rank, leaf = basis_ref.shape
    vecs = out_ref.shape[0]
    lower = 2 * leaf_count - 2
    npts = leaf_count * leaf
    nskel = lower * rank
    offsets, counts = level_table(leaf_count)
    up_offsets, up_counts = level_table(n)

    def features(p):
        q = (p - 0.5) * point_scale
        high = q.astype(bf16).astype(f32)
        low = (q - high).astype(bf16).astype(f32)
        q = high + low
        norm = jnp.sum(q * q, axis=0, keepdims=True)
        n1 = norm.astype(bf16).astype(f32)
        n2 = (norm - n1).astype(bf16).astype(f32)
        n3 = norm - n1 - n2
        return high, low, n1, n2, n3

    def put(p, width):
        high, low, n1, n2, n3 = features(p)
        span = slice(0, width)
        one = jnp.ones((1, width), f32)
        for k, rows in enumerate((high, low, high, low)):
            feat[0, 3 * k : 3 * k + 3, span] = -2.0 * rows
        for k, rows in enumerate((high, high, low, low)):
            feat[1, 3 * k : 3 * k + 3, span] = rows
        for k, rows in enumerate((n1, n2, n3, one, one, one)):
            feat[0, 12 + k : 13 + k, span] = rows
        for k, rows in enumerate((one, one, one, n1, n2, n3)):
            feat[1, 12 + k : 13 + k, span] = rows

    def columns_to(target, first, start, width):
        for t in range(width // 128):
            tile = feat[0, :, start + t * 128 : start + (t + 1) * 128]
            target[first + t * 128 : first + (t + 1) * 128, :] = tile.T.astype(bf16)

    def rows_to(target, start, nodes):
        for j in range(nodes):
            target[j] = feat[1, :, start + j * rank : start + (j + 1) * rank].astype(bf16)

    feat[...] = jnp.zeros(feat.shape, f32)
    for slot in range(3):
        put(ptsall[slot], npts + nskel)
        columns_to(near_t, slot * npts, 0, npts)
        columns_to(skel_t, slot * nskel, npts, nskel)
        if slot == 1:
            near_row[...] = feat[1, :, 0:npts].astype(bf16)
            rows_to(skel_row, npts, lower)

    chunk = math.gcd(uppts_ref.shape[1], 1024)

    def up_chunk(i):
        base = i * chunk if isinstance(i, int) else pl.multiple_of(i * chunk, chunk)
        put(uppts_ref[:, pl.ds(base, chunk)], chunk)
        for t in range(chunk // 128):
            tile = feat[0, :, t * 128 : (t + 1) * 128]
            up_t[pl.ds(base + t * 128, 128), :] = tile.T.astype(bf16)
        for j in range(chunk // rank):
            up_row[i * (chunk // rank) + j] = feat[1, :, j * rank : (j + 1) * rank].astype(bf16)

    each(0, uppts_ref.shape[1] // chunk, up_chunk)

    def load_roots(j):
        upc[j] = roots[j, 0:vecs, 0:rank]

    each(0, n, load_roots)

    def first_lift(j):
        upc[n + j] = roots[2 * j, 0:vecs, rank : 2 * rank] + roots[2 * j + 1, 0:vecs, rank : 2 * rank]

    each(0, n // 2, first_lift)
    for height in range(2, len(up_counts)):

        def lift(j, height=height):
            child = up_offsets[height - 1] + 2 * j
            upc[up_offsets[height] + j] = dot_nt(upc[child], uptr_ref[child - n]) + dot_nt(
                upc[child + 1], uptr_ref[child + 1 - n]
            )

        each(0, up_counts[height], lift)

    pair_rows = roots[:, vecs, :]
    pair_cols = roots[:, vecs + 1, :]
    used = lax.broadcasted_iota(jnp.int32, pair_rows.shape, 1) < entries
    value = None
    for height in range(len(up_counts) - 1, -1, -1):
        node = up_offsets[height] + lax.div(me, 2**height)
        mine = jnp.logical_and(pair_rows == node.astype(f32), used)
        row_feat = up_row[node]

        def term(c, mine=mine, row_feat=row_feat):
            named = jnp.logical_and(mine, pair_cols == jnp.asarray(c, f32))
            times = jnp.sum(jnp.sum(jnp.where(named, ln2, 0.0), axis=1, keepdims=True), axis=0, keepdims=True)
            start = c * rank if isinstance(c, int) else pl.multiple_of(c * rank, rank)
            kernel = kernel_values(dot_fast(up_t[pl.ds(start, rank), :], row_feat))
            return product(upc[c] * times, kernel)

        first = up_offsets[height]
        if up_counts[height] <= 16:
            level = sum(term(first + j) for j in range(up_counts[height]))
        else:
            level = lax.fori_loop(
                0,
                up_counts[height],
                lambda j, acc: acc + term(first + j),
                jnp.zeros((vecs, rank), f32),
            )
        if value is not None:
            if height == 0:
                level = level + dot_nn(value, tr_ref[lower])
            else:
                level = level + dot_nn(value, uptr_ref[node - n])
        value = level

    y_ref[...] = jnp.zeros(y_ref.shape, f32)
    y_ref[lower] = value * (1.0 / ln2)

    far_total = far_ref.shape[1]
    far_group = math.gcd(far_total, 4)

    @pl.loop(0, far_total // far_group)
    def _(g):
        done = []
        for k in range(far_group):
            r = far_ref[0, g * far_group + k]
            c = far_ref[1, g * far_group + k]
            squared = dot_fast(skel_t[pl.ds(pl.multiple_of(c * rank, rank), rank), :], skel_row[r])
            done.append((r, product(call[c], kernel_values(squared))))
        for r, part in done:
            y_ref[r] += part

    for height in range(len(counts) - 2, -1, -1):
        for j in range(counts[height]):
            node = offsets[height] + j
            y_ref[node] += dot_nn(y_ref[offsets[height + 1] + j // 2], tr_ref[node])

    @pl.loop(0, leaf_count)
    def _(r):
        lanes = pl.ds(pl.multiple_of(r * leaf, leaf), leaf)
        row_feat = near_row[:, lanes]
        groups = lax.div(cols_ref[r, 127] + (GROUP - 1), GROUP)

        def near_group(g, acc):
            values = []
            places = []
            for k in range(GROUP):
                c = cols_ref[r, g * GROUP + k]
                slot = lax.div(c, leaf_count)
                inside = pl.multiple_of((c - slot * leaf_count) * leaf, leaf)
                values.append(xall[slot, :, pl.ds(inside, leaf)] * wts_ref[r, g * GROUP + k])
                places.append(near_t[pl.ds(pl.multiple_of(c * leaf, leaf), leaf), :])
            kernel = kernel_values(dot_fast(jnp.concatenate(places, axis=0), row_feat))
            return acc + product(jnp.concatenate(values, axis=1), kernel)

        acc = lax.fori_loop(0, groups, near_group, jnp.zeros((vecs, leaf), f32))
        out_ref[:, lanes] = acc + dot_nn(y_ref[r] * ln2, basis_ref[r])


def per_device(
    vectors,
    points,
    leaf_basis,
    local_transfer,
    local_skeleton,
    upper_transfer,
    upper_skeleton,
    near_list,
    far_list,
    upper_list,
):
    leaf_count, rank, leaf = leaf_basis.shape
    vecs, npts = vectors.shape
    n = lax.axis_size("leaf")
    lower = 2 * leaf_count - 2
    nskel = lower * rank
    halo_width = npts + nskel
    nup = 2 * n * rank
    vmem = pl.BlockSpec(memory_space=pltpu.VMEM)
    smem = pl.BlockSpec(memory_space=pltpu.SMEM)
    pts = jnp.concatenate(
        [points, jnp.transpose(local_skeleton, (1, 0, 2)).reshape(3, nskel)], axis=1
    )
    uppts = jnp.pad(
        jnp.transpose(upper_skeleton, (1, 0, 2)).reshape(3, (2 * n - 1) * rank), ((0, 0), (0, rank))
    )
    root_rows = vecs + 8
    xall, ptsall, call, roots, cols, wts = pl.pallas_call(
        functools.partial(exchange_kernel, n, halo_width),
        out_shape=(
            jax.ShapeDtypeStruct((3, vecs, npts), f32),
            jax.ShapeDtypeStruct((3, 3, halo_width), f32),
            jax.ShapeDtypeStruct((3 * lower, vecs, rank), f32),
            jax.ShapeDtypeStruct((n, root_rows, 2 * rank), f32),
            jax.ShapeDtypeStruct((leaf_count, 128), jnp.int32),
            jax.ShapeDtypeStruct((leaf_count, 128), f32),
        ),
        in_specs=[vmem] * 6,
        out_specs=(vmem,) * 6,
        scratch_shapes=[
            pltpu.SemaphoreType.DMA((3, 2)),
            pltpu.SemaphoreType.DMA((3, 2)),
            pltpu.SemaphoreType.DMA((n,)),
            pltpu.SemaphoreType.DMA((n,)),
        ],
        compiler_params=pltpu.CompilerParams(
            collective_id=0, has_side_effects=True, vmem_limit_bytes=40 * 2**20
        ),
    )(vectors, pts, leaf_basis, local_transfer, upper_list, near_list)
    return pl.pallas_call(
        functools.partial(couple_kernel, n, upper_list.shape[1]),
        out_shape=jax.ShapeDtypeStruct((vecs, npts), f32),
        in_specs=[smem] * 3 + [vmem] * 8,
        out_specs=vmem,
        scratch_shapes=[
            pltpu.VMEM((2, FEATURES, halo_width), f32),
            pltpu.VMEM((3 * npts, FEATURES), bf16),
            pltpu.VMEM((FEATURES, npts), bf16),
            pltpu.VMEM((3 * nskel, FEATURES), bf16),
            pltpu.VMEM((lower, FEATURES, rank), bf16),
            pltpu.VMEM((nup, FEATURES), bf16),
            pltpu.VMEM((2 * n, FEATURES, rank), bf16),
            pltpu.VMEM((lower + 1, vecs, rank), f32),
            pltpu.VMEM((2 * n, vecs, rank), f32),
        ],
        compiler_params=pltpu.CompilerParams(vmem_limit_bytes=48 * 2**20),
    )(cols, wts, far_list, xall, ptsall, uppts, call, roots, leaf_basis, local_transfer, upper_transfer)


def solution(mesh):
    return jax.shard_map(
        per_device,
        mesh=mesh,
        in_specs=(
            P("sub", ("groups", "leaf")),
            P(None, ("groups", "leaf")),
            P(("groups", "leaf"), None, None),
            P(("groups", "leaf"), None, None),
            P(("groups", "leaf"), None, None),
            P(),
            P(),
            P(None, ("groups", "leaf")),
            P(None, ("groups", "leaf")),
            P(None, ("groups", "leaf")),
        ),
        out_specs=P("sub", ("groups", "leaf")),
        check_vma=False,
    )
```

time: 293 us -> 98.9 us (0.34)
  blocking collectives: 105 us -> 0 us
  Pallas kernels: 0 us -> 92.6 us
  matrix products: 82.1 us -> 0 us
  other arithmetic: 68.3 us -> 0.02 us
  local copies, waits for them, and re-layouts: 22.5 us -> 4.52 us
  starting transfers between devices: 12.8 us -> 0 us
    pallas_call x0 -> x2, Pallas kernels: none -> 92.6 us  [the longest x1 66.5 us: per_device(): pl.pallas_call(functools.partial(couple_kernel, n, upper_list.shape[1]),...]
    dot_general x26 -> x0, matrix products: 82.1 us -> none  [the longest x8 60.8 us: near_add_block(): jnp.einsum('gij,vgj->vgi', kernel, sources[3:], precision=highest)]
    all_gather x2 -> x0, blocking collectives: 70.2 us -> none  [the longest x1 39.6 us: per_device(): lax.all_gather(root_coef[None], 'leaf', axis=0, tiled=True)]
    psum x1 -> x0, blocking collectives: 34.8 us -> none  [per_device(): upper_y = lax.psum(upper_share, 'leaf')]
    reduce_sum x11 -> x0, other arithmetic: 34.5 us -> none  [the longest x10 34.4 us: matern(): jnp.sum(separation * separation, axis=-3)]
    scatter-add x10 -> x0, other arithmetic: 29.8 us -> none  [the longest x8 23.4 us: near_add_block(): return (running.at[:, row_block].add(products), None)]
    gather x26 -> x0, local copies, waits for them, and re-layouts: 14.7 us -> none  [the longest x8 5.25 us: near_add_block(): own_points[:, row_block]]
    ppermute x4 -> x0, starting transfers between devices: 12.8 us -> none  [the longest x2 10.2 us: extended(): lax.ppermute(tail, axis, [(i, (i + 1) % count) for i in range(ends)])]
  transfers between devices with their start and end apart: 4 -> 0, of which waited for: 0 -> 0; matrix products, arithmetic and copies ran while one was open for 12% -> 0% of each run, Pallas kernels for 0% -> 0%
where the time goes in v1:
time: 98.9 us; the launch traced here: 97.3 us
  Pallas kernels  92.6 us (94%)
  local copies, waits for them, and re-layouts  4.52 us (5%)
    pallas_call x1, Pallas kernels, per_device(): pl.pallas_call(functools.partial(couple_kernel, n, upper_list.shape[1]),...  66.5 us
    pallas_call x1, Pallas kernels, per_device(): pl.pallas_call(functools.partial(exchange_kernel, n, halo_width), out_sha...  26.1 us
    unnamed x22, local copies, waits for them, and re-layouts  3.57 us

profile of v1, /device:TPU:0, one launch (start us, length us, event | category | flops | bytes accessed | tf_op | source)
XLA Modules:
  0.0 97.3 jit_solution(17370744530115848319)
XLA Ops:
  0.0 0.0 copy-start.9
  0.0 0.0 copy-start.10
  0.0 0.0 copy-start.5
  0.0 0.9 reshape.7
  0.9 0.0 copy-done.9
  0.9 0.1 reshape.6
  1.0 0.0 copy-done.10
  1.0 0.0 copy-start.6
  1.0 0.0 copy-start.7
  1.0 0.0 copy-done.5
  1.0 0.6 copy-done.6
  1.7 0.0 copy-done.7
  1.7 0.0 copy-start
  1.7 1.2 %copy-done = f32[31,64,64]{2,1,0:T(8,128)S(1)} copy-done((f32[31,64,64]{2,1,0:T(8,128)S(1)}, f32[31,64,64]{2,1,0:T(8,128)}, u32[]{:S(2)}) %copy-start) | copy-done | bytes 507928
  2.9 0.0 copy-start.2
  2.9 1.0 %copy-done.2 = f32[16,64,128]{2,1,0:T(8,128)S(1)} copy-done((f32[16,64,128]{2,1,0:T(8,128)S(1)}, f32[16,64,128]{2,1,0:T(8,128)}, u32[]{:S(2)}) %copy-start.2) | copy-done | bytes 524312
  3.9 0.0 copy-start.1
  3.9 0.0 copy-start.3
  3.9 0.0 copy-start.4
  3.9 26.1 %shard_map.100 = (f32[3,16,2048]{2,1,0:T(8,128)S(1)}, f32[3,3,3968]{2,1,0:T(4,128)S(1)}, f32[90,16,64]{2,1,0:T(8,128)S(1)}, f32[8,24,128]{2,1,0:T(8,128)S(1)}, s...) custom-call(f32[16,2048]{1,0:T(8,128)S(1)} %copy-done.5, f32[3,3968]{1,0:T(4,128)S(1)} %pad_maximum_fusion.pts_ref, ...), custom_call_target="tpu_custom_call" | custom-call | tf_op jit(solution)/shard_map/pallas_call | solution.py:466
  30.1 0.0 copy-start.8
  30.1 0.0 copy-done.1
  30.1 0.0 copy-done.3
  30.1 0.0 copy-done.4
  30.1 0.6 copy-done.8
  30.8 66.5 %shard_map.101 = f32[16,2048]{1,0:T(8,128)} custom-call(s32[16,128]{1,0:T(8,128)S(1)} %get-tuple-element.11.cols_ref, f32[16,128]{1,0:T(8,128)S(1)} %get-tuple-element.12.wts_ref, s32[2,128]{1,0:T(2,128)S(1)} %copy-done.8, f32[3,16,2048]{2,1,0:T(8,128)S(1)} %get-tuple-element.13.xall, f32[3,3,3968]{2,1,0:T(4,128)S(1)} %get-tuple-element.14.ptsall, ...), custom_call_target="tpu_custom_call" | custom-call | tf_op jit(solution)/shard_map/pallas_call | solution.py:488
  (2 shorter events, 0.0 us)
Async XLA Ops:
  0.0 0.9 copy-start.9
  0.0 1.0 copy-start.10
  0.0 1.0 %copy-start.5 = (f32[16,2048]{1,0:T(8,128)S(1)}, f32[16,2048]{1,0:T(8,128)}, u32[]{:S(2)}) copy-start(f32[16,2048]{1,0:T(8,128)} %x_ref.1) | copy-start | bytes 393220
  1.0 0.7 copy-start.6
  1.0 0.7 copy-start.7
  1.7 1.2 %copy-start = (f32[31,64,64]{2,1,0:T(8,128)S(1)}, f32[31,64,64]{2,1,0:T(8,128)}, u32[]{:S(2)}) copy-start(f32[31,64,64]{2,1,0:T(8,128)} %tr_ref.3) | copy-start | bytes 1523716
  2.9 1.0 %copy-start.2 = (f32[16,64,128]{2,1,0:T(8,128)S(1)}, f32[16,64,128]{2,1,0:T(8,128)}, u32[]{:S(2)}) copy-start(f32[16,64,128]{2,1,0:T(8,128)} %basis_ref.3) | copy-start | bytes 1572868
  3.9 26.2 %copy-start.1 = (f32[31,64,64]{2,1,0:T(8,128)S(1)}, f32[31,64,64]{2,1,0:T(8,128)}, u32[]{:S(2)}) copy-start(f32[31,64,64]{2,1,0:T(8,128)} %tr_ref.3) | copy-start | bytes 1523716
  3.9 26.2 %copy-start.3 = (f32[16,64,128]{2,1,0:T(8,128)S(1)}, f32[16,64,128]{2,1,0:T(8,128)}, u32[]{:S(2)}) copy-start(f32[16,64,128]{2,1,0:T(8,128)} %basis_ref.3) | copy-start | bytes 1572868
  3.9 26.2 %copy-start.4 = (f32[6,64,64]{2,1,0:T(8,128)S(1)}, f32[6,64,64]{2,1,0:T(8,128)}, u32[]{:S(2)}) copy-start(f32[6,64,64]{2,1,0:T(8,128)} %uptr_ref.1) | copy-start | bytes 294916
  30.1 0.7 copy-start.8

commit v2 on v1

--- a/solution.py
+++ b/solution.py
@@ -16,7 +16,8 @@
 highest = lax.Precision.HIGHEST
 MESH = pl.DeviceIdType.MESH
 FEATURES = 32
-GROUP = 4
+GROUP = 16
+FAR_GROUP = 16
 f32 = jnp.float32
 bf16 = jnp.bfloat16
 
@@ -72,7 +73,7 @@
     nlist_ref,
     xall,
     ptsall,
-    call,
+    packed,
     roots,
     cols_out,
     wts_out,
@@ -80,6 +81,7 @@
     halo_recv,
     root_send,
     root_recv,
+    call,
 ):
     me = lax.axis_index("leaf")
     leaf_count, rank, leaf = basis_ref.shape
@@ -99,12 +101,12 @@
     pl.semaphore_wait(barrier, n - 1)
 
     own_pts = pts_ref.at[:, pl.ds(0, halo_width)]
-    own_coefs = call.at[pl.ds(lower, lower)]
+    own_coefs = packed.at[1]
     sources = (x_ref, own_pts, own_coefs)
 
     def halo(kind, side):
         slot = 2 * side
-        target = (xall.at[slot], ptsall.at[slot], call.at[pl.ds(slot * lower, lower)])[kind]
+        target = (xall.at[slot], ptsall.at[slot], packed.at[slot])[kind]
         other = jnp.minimum(me + 1, n - 1) if side == 0 else jnp.maximum(me - 1, 0)
         return pltpu.make_async_remote_copy(
             src_ref=sources[kind],
@@ -129,14 +131,19 @@
             halo(1, side).start()
 
     def up(node):
-        return dot_nt(call[lower + node], tr_ref[node])
+        return dot_nt(call[node], tr_ref[node])
+
+    def keep(node, value):
+        call[node] = value
+        half = node % 2 * rank
+        packed[1, node // 2, :, half : half + rank] = value
 
     for i in range(leaf_count):
-        call[lower + i] = dot_nt(x_ref[:, i * leaf : (i + 1) * leaf], basis_ref[i])
+        keep(i, dot_nt(x_ref[:, i * leaf : (i + 1) * leaf], basis_ref[i]))
     for height in range(1, len(counts) - 1):
         below = offsets[height - 1]
         for j in range(counts[height]):
-            call[lower + offsets[height] + j] = up(below + 2 * j) + up(below + 2 * j + 1)
+            keep(offsets[height] + j, up(below + 2 * j) + up(below + 2 * j + 1))
     for side in range(2):
 
         @pl.when(sends(side))
@@ -181,7 +188,7 @@
         def _():
             xall[slot] = jnp.zeros(xall.shape[1:], f32)
             ptsall[slot] = jnp.zeros(ptsall.shape[1:], f32)
-            call[slot * lower : (slot + 1) * lower] = jnp.zeros((lower,) + call.shape[1:], f32)
+            packed[slot] = jnp.zeros(packed.shape[1:], f32)
 
     total = nlist_ref.shape[1]
     row_hot = (
@@ -259,7 +266,7 @@
     xall,
     ptsall,
     uppts_ref,
-    call,
+    packed,
     roots,
     basis_ref,
     tr_ref,
@@ -274,6 +281,7 @@
     up_row,
     y_ref,
     upc,
+    call,
 ):
     me = lax.axis_index("leaf")
     leaf_count, rank, leaf = basis_ref.shape
@@ -313,10 +321,6 @@
             tile = feat[0, :, start + t * 128 : start + (t + 1) * 128]
             target[first + t * 128 : first + (t + 1) * 128, :] = tile.T.astype(bf16)
 
-    def rows_to(target, start, nodes):
-        for j in range(nodes):
-            target[j] = feat[1, :, start + j * rank : start + (j + 1) * rank].astype(bf16)
-
     feat[...] = jnp.zeros(feat.shape, f32)
     for slot in range(3):
         put(ptsall[slot], npts + nskel)
@@ -324,7 +328,11 @@
         columns_to(skel_t, slot * nskel, npts, nskel)
         if slot == 1:
             near_row[...] = feat[1, :, 0:npts].astype(bf16)
-            rows_to(skel_row, npts, lower)
+            skel_row[...] = jnp.zeros(skel_row.shape, bf16)
+            for j in range(lower):
+                tile = feat[1, :, npts + j * rank : npts + (j + 1) * rank].astype(bf16)
+                for h in range(2):
+                    skel_row[2 * j + h, :, h * rank : (h + 1) * rank] = tile
 
     chunk = math.gcd(uppts_ref.shape[1], 1024)
 
@@ -394,19 +402,43 @@
     y_ref[...] = jnp.zeros(y_ref.shape, f32)
     y_ref[lower] = value * (1.0 / ln2)
 
+    for slot in range(3):
+        for j in range(lower):
+            half = j % 2 * rank
+            call[slot * lower + j] = packed[slot, j // 2, :, half : half + rank]
     far_total = far_ref.shape[1]
-    far_group = math.gcd(far_total, 4)
+    far_group = math.gcd(far_total, FAR_GROUP)
 
     @pl.loop(0, far_total // far_group)
     def _(g):
-        done = []
+        named = [
+            (far_ref[0, g * far_group + k], far_ref[1, g * far_group + k]) for k in range(far_group)
+        ]
+        tiles = []
+        for k in range(0, far_group, 2):
+            tiles.append(
+                sum(
+                    dot_fast(
+                        skel_t[pl.ds(pl.multiple_of(named[k + h][1] * rank, rank), rank), :],
+                        skel_row[2 * named[k + h][0] + h],
+                    )
+                    for h in range(2)
+                )
+            )
+        kernel_high, kernel_low = split(kernel_values(jnp.concatenate(tiles, axis=0)))
+        parts = []
+        for k in range(0, far_group, 2):
+            rows = slice(k // 2 * rank, (k // 2 + 1) * rank)
+            high, low = split(
+                jnp.concatenate([call[named[k][1]], call[named[k + 1][1]]], axis=0)
+            )
+            both = dot_fast(jnp.concatenate([high, low], axis=0), kernel_high[rows])
+            parts.append(
+                both[: 2 * vecs] + both[2 * vecs :] + dot_fast(high, kernel_low[rows])
+            )
         for k in range(far_group):
-            r = far_ref[0, g * far_group + k]
-            c = far_ref[1, g * far_group + k]
-            squared = dot_fast(skel_t[pl.ds(pl.multiple_of(c * rank, rank), rank), :], skel_row[r])
-            done.append((r, product(call[c], kernel_values(squared))))
-        for r, part in done:
-            y_ref[r] += part
+            h = k % 2
+            y_ref[named[k][0]] += parts[k // 2][h * vecs : (h + 1) * vecs, h * rank : (h + 1) * rank]
 
     for height in range(len(counts) - 2, -1, -1):
         for j in range(counts[height]):
@@ -417,21 +449,28 @@
     def _(r):
         lanes = pl.ds(pl.multiple_of(r * leaf, leaf), leaf)
         row_feat = near_row[:, lanes]
-        groups = lax.div(cols_ref[r, 127] + (GROUP - 1), GROUP)
-
-        def near_group(g, acc):
+        filled = cols_ref[r, 127]
+        wide = lax.div(filled + (GROUP // 2 - 1), GROUP)
+        narrow = lax.div(jnp.maximum(filled - wide * GROUP, 0) + (GROUP // 2 - 1), GROUP // 2)
+
+        def near_group(first, size, acc):
             values = []
             places = []
-            for k in range(GROUP):
-                c = cols_ref[r, g * GROUP + k]
+            for k in range(size):
+                c = cols_ref[r, first + k]
                 slot = lax.div(c, leaf_count)
                 inside = pl.multiple_of((c - slot * leaf_count) * leaf, leaf)
-                values.append(xall[slot, :, pl.ds(inside, leaf)] * wts_ref[r, g * GROUP + k])
+                values.append(xall[slot, :, pl.ds(inside, leaf)] * wts_ref[r, first + k])
                 places.append(near_t[pl.ds(pl.multiple_of(c * leaf, leaf), leaf), :])
             kernel = kernel_values(dot_fast(jnp.concatenate(places, axis=0), row_feat))
             return acc + product(jnp.concatenate(values, axis=1), kernel)
 
-        acc = lax.fori_loop(0, groups, near_group, jnp.zeros((vecs, leaf), f32))
+        acc = lax.fori_loop(
+            0, wide, lambda g, acc: near_group(g * GROUP, GROUP, acc), jnp.zeros((vecs, leaf), f32)
+        )
+        acc = lax.fori_loop(
+            0, narrow, lambda g, acc: near_group(wide * GROUP, GROUP // 2, acc), acc
+        )
         out_ref[:, lanes] = acc + dot_nn(y_ref[r] * ln2, basis_ref[r])
 
 
@@ -463,12 +502,12 @@
         jnp.transpose(upper_skeleton, (1, 0, 2)).reshape(3, (2 * n - 1) * rank), ((0, 0), (0, rank))
     )
     root_rows = vecs + 8
-    xall, ptsall, call, roots, cols, wts = pl.pallas_call(
+    xall, ptsall, packed, roots, cols, wts = pl.pallas_call(
         functools.partial(exchange_kernel, n, halo_width),
         out_shape=(
             jax.ShapeDtypeStruct((3, vecs, npts), f32),
             jax.ShapeDtypeStruct((3, 3, halo_width), f32),
-            jax.ShapeDtypeStruct((3 * lower, vecs, rank), f32),
+            jax.ShapeDtypeStruct((3, lower // 2, vecs, 2 * rank), f32),
             jax.ShapeDtypeStruct((n, root_rows, 2 * rank), f32),
             jax.ShapeDtypeStruct((leaf_count, 128), jnp.int32),
             jax.ShapeDtypeStruct((leaf_count, 128), f32),
@@ -480,6 +519,7 @@
             pltpu.SemaphoreType.DMA((3, 2)),
             pltpu.SemaphoreType.DMA((n,)),
             pltpu.SemaphoreType.DMA((n,)),
+            pltpu.VMEM((lower, vecs, rank), f32),
         ],
         compiler_params=pltpu.CompilerParams(
             collective_id=0, has_side_effects=True, vmem_limit_bytes=40 * 2**20
@@ -495,14 +535,15 @@
             pltpu.VMEM((3 * npts, FEATURES), bf16),
             pltpu.VMEM((FEATURES, npts), bf16),
             pltpu.VMEM((3 * nskel, FEATURES), bf16),
-            pltpu.VMEM((lower, FEATURES, rank), bf16),
+            pltpu.VMEM((2 * lower, FEATURES, 2 * rank), bf16),
             pltpu.VMEM((nup, FEATURES), bf16),
             pltpu.VMEM((2 * n, FEATURES, rank), bf16),
             pltpu.VMEM((lower + 1, vecs, rank), f32),
             pltpu.VMEM((2 * n, vecs, rank), f32),
+            pltpu.VMEM((3 * lower, vecs, rank), f32),
         ],
         compiler_params=pltpu.CompilerParams(vmem_limit_bytes=48 * 2**20),
-    )(cols, wts, far_list, xall, ptsall, uppts, call, roots, leaf_basis, local_transfer, upper_transfer)
+    )(cols, wts, far_list, xall, ptsall, uppts, packed, roots, leaf_basis, local_transfer, upper_transfer)
 
 
 def solution(mesh):

time: 98.9 us -> 57.7 us (0.58); the launches traced: 97.3 us -> 57.3 us
  Pallas kernels: 92.6 us -> 52.7 us
    pallas_call x1, Pallas kernels: 66.5 us -> 31.8 us  [per_device(): pl.pallas_call(functools.partial(couple_kernel, n, upper_list.shape[1]),...]
    pallas_call x1, Pallas kernels: 26.1 us -> 20.9 us  [per_device(): pl.pallas_call(functools.partial(exchange_kernel, n, halo_width), out_sha...]
where the time goes in v2:
time: 57.7 us; the launch traced here: 57.3 us
  Pallas kernels  52.7 us (91%)
  local copies, waits for them, and re-layouts  4.52 us (8%)
    pallas_call x1, Pallas kernels, per_device(): pl.pallas_call(functools.partial(couple_kernel, n, upper_list.shape[1]),...  31.8 us
    pallas_call x1, Pallas kernels, per_device(): pl.pallas_call(functools.partial(exchange_kernel, n, halo_width), out_sha...  20.9 us
    unnamed x22, local copies, waits for them, and re-layouts  3.57 us

profile of v2, /device:TPU:0, one launch (start us, length us, event | category | flops | bytes accessed | tf_op | source)
XLA Modules:
  0.0 57.3 jit_solution(9716642554867792804)
XLA Ops:
  0.0 0.0 copy-start.9
  0.0 0.0 copy-start.10
  0.0 0.0 copy-start.5
  0.0 0.9 %reshape.7 = f32[3,960]{1,0:T(4,128)S(1)} reshape(f32[3,15,64]{2,1,0:T(8,128)} %bitcast.3) | data formatting | bytes 23040 | tf_op jit(solution)/shard_map/reshape | solution.py:502
  0.9 0.0 copy-done.9
  0.9 0.1 reshape.6
  1.0 0.0 copy-done.10
  1.0 0.0 copy-start.6
  1.0 0.0 copy-start.7
  1.0 0.0 copy-done.5
  1.0 0.6 %copy-done.6 = s32[2,512]{1,0:T(2,128)S(1)} copy-done((s32[2,512]{1,0:T(2,128)S(1)}, s32[2,512]{1,0:T(2,128)}, u32[]{:S(2)}) %copy-start.6) | copy-done | bytes 4120
  1.7 0.0 copy-done.7
  1.7 0.0 copy-start
  1.7 1.2 %copy-done = f32[31,64,64]{2,1,0:T(8,128)S(1)} copy-done((f32[31,64,64]{2,1,0:T(8,128)S(1)}, f32[31,64,64]{2,1,0:T(8,128)}, u32[]{:S(2)}) %copy-start) | copy-done | bytes 507928
  2.9 0.0 copy-start.2
  2.9 1.0 %copy-done.2 = f32[16,64,128]{2,1,0:T(8,128)S(1)} copy-done((f32[16,64,128]{2,1,0:T(8,128)S(1)}, f32[16,64,128]{2,1,0:T(8,128)}, u32[]{:S(2)}) %copy-start.2) | copy-done | bytes 524312
  3.9 0.0 copy-start.1
  3.9 0.0 copy-start.3
  3.9 0.0 copy-start.4
  3.9 20.9 %shard_map.100 = (f32[3,16,2048]{2,1,0:T(8,128)S(1)}, f32[3,3,3968]{2,1,0:T(4,128)S(1)}, f32[3,15,16,128]{3,2,1,0:T(8,128)S(1)}, f32[8,24,128]{2,1,0:T(8,128)S(1...) custom-call(f32[16,2048]{1,0:T(8,128)S(1)} %copy-done.5, f32[3,3968]{1,0:T(4,128)S(1)} %pad_maximum_fusion.pts_ref, ...), custom_call_target="tpu_custom_call" | custom-call | tf_op jit(solution)/shard_map/pallas_call | solution.py:505
  24.8 0.0 copy-start.8
  24.8 0.0 copy-done.1
  24.8 0.0 copy-done.3
  24.8 0.0 copy-done.4
  24.8 0.6 %copy-done.8 = s32[2,128]{1,0:T(2,128)S(1)} copy-done((s32[2,128]{1,0:T(2,128)S(1)}, s32[2,128]{1,0:T(2,128)}, u32[]{:S(2)}) %copy-start.8) | copy-done | bytes 1048
  25.5 31.8 %shard_map.101 = f32[16,2048]{1,0:T(8,128)} custom-call(s32[16,128]{1,0:T(8,128)S(1)} %get-tuple-element.11.cols_ref, f32[16,128]{1,0:T(8,128)S(1)} %get-tuple-element.12.wts_ref, s32[2,128]{1,0:T(2,128)S(1)} %copy-done.8, f32[3,16,2048]{2,1,0:T(8,128)S(1)} %get-tuple-element.13.xall, f32[3,3,3968]{2,1,0:T(4,128)S(1)} %get-tuple-element.14.ptsall, ...), custom_call_target="tpu_custom_call" | custom-call | tf_op jit(solution)/shard_map/pallas_call | solution.py:528
  (2 shorter events, 0.0 us)
Async XLA Ops:
  0.0 0.9 %copy-start.9 = (f32[30,3,64]{2,0,1:T(8,128)S(1)}, f32[30,3,64]{2,0,1:T(8,128)}, u32[]{:S(2)}) copy-start(f32[30,3,64]{2,0,1:T(8,128)} %param.14) | copy-start | bytes 69124
  0.0 1.0 %copy-start.10 = (f32[3,2048]{1,0:T(4,128)S(1)}, f32[3,2048]{1,0:T(4,128)}, u32[]{:S(2)}) copy-start(f32[3,2048]{1,0:T(4,128)} %param.11) | copy-start | bytes 73732
  0.0 1.0 %copy-start.5 = (f32[16,2048]{1,0:T(8,128)S(1)}, f32[16,2048]{1,0:T(8,128)}, u32[]{:S(2)}) copy-start(f32[16,2048]{1,0:T(8,128)} %x_ref.1) | copy-start | bytes 393220
  1.0 0.7 %copy-start.6 = (s32[2,512]{1,0:T(2,128)S(1)}, s32[2,512]{1,0:T(2,128)}, u32[]{:S(2)}) copy-start(s32[2,512]{1,0:T(2,128)} %nlist_ref.1) | copy-start | bytes 12292
  1.0 0.7 %copy-start.7 = (s32[2,16]{1,0:T(2,128)S(1)}, s32[2,16]{1,0:T(2,128)}, u32[]{:S(2)}) copy-start(s32[2,16]{1,0:T(2,128)} %ulist_ref.1) | copy-start | bytes 388
  1.7 1.2 %copy-start = (f32[31,64,64]{2,1,0:T(8,128)S(1)}, f32[31,64,64]{2,1,0:T(8,128)}, u32[]{:S(2)}) copy-start(f32[31,64,64]{2,1,0:T(8,128)} %tr_ref.3) | copy-start | bytes 1523716
  2.9 1.0 %copy-start.2 = (f32[16,64,128]{2,1,0:T(8,128)S(1)}, f32[16,64,128]{2,1,0:T(8,128)}, u32[]{:S(2)}) copy-start(f32[16,64,128]{2,1,0:T(8,128)} %basis_ref.3) | copy-start | bytes 1572868
  3.9 20.9 %copy-start.1 = (f32[31,64,64]{2,1,0:T(8,128)S(1)}, f32[31,64,64]{2,1,0:T(8,128)}, u32[]{:S(2)}) copy-start(f32[31,64,64]{2,1,0:T(8,128)} %tr_ref.3) | copy-start | bytes 1523716
  3.9 20.9 %copy-start.3 = (f32[16,64,128]{2,1,0:T(8,128)S(1)}, f32[16,64,128]{2,1,0:T(8,128)}, u32[]{:S(2)}) copy-start(f32[16,64,128]{2,1,0:T(8,128)} %basis_ref.3) | copy-start | bytes 1572868
  3.9 20.9 %copy-start.4 = (f32[6,64,64]{2,1,0:T(8,128)S(1)}, f32[6,64,64]{2,1,0:T(8,128)}, u32[]{:S(2)}) copy-start(f32[6,64,64]{2,1,0:T(8,128)} %uptr_ref.1) | copy-start | bytes 294916
  24.8 0.7 %copy-start.8 = (s32[2,128]{1,0:T(2,128)S(1)}, s32[2,128]{1,0:T(2,128)}, u32[]{:S(2)}) copy-start(s32[2,128]{1,0:T(2,128)} %far_ref.1) | copy-start | bytes 3076
